TPU v7x, 32 devices: a whole 2x2x4 slice. The times are simulated.
32 devices in a mesh: rows: 8 (over z, x), cols: 4 (over y, core).
Axes of the slice: x: 2, y: 2, z: 4, core: 2. Of those that a mesh axis runs over, the one named last changes fastest.
Arguments:
- trailing: float32 [8192, 4096], P('rows', 'cols'), may hold values from -6 to 6
- leaf_v: float32 [8192, 512], P('rows', 'cols'), may hold values from -0.1875 to 0.1875
- leaf_t: float32 [4096, 512], P('rows', 'cols'), may hold values from -0.25 to 0.25
- merge_v: float32 [8192, 512], P('rows'), may hold values from -0.1875 to 0.1875
- merge_t: float32 [4096, 512], P('rows'), may hold values from -0.25 to 0.25
Outputs:
- updated: float32 [8192, 4096], P('rows', 'cols')
All inputs are finite; a program needn't handle non-finite values.
Results may differ from a plain program's by a relative error of at most 0.00011.
Values sent between devices are 32-bit elements; how exact they have to be, the bound alone decides.
A program may use at most 128 MiB of HBM per device.

v0:
```python
import jax
import jax.numpy as jnp
from jax import lax
from jax.sharding import PartitionSpec as P


def partner(block, axis, apart):
    count = lax.axis_size(axis)
    route = []
    for low in range(count):
        high = low | 1 << apart
        if high != low and high < count:
            route += [(low, high), (high, low)]
    return lax.ppermute(block, axis, route)


def mult(left, right):
    return jnp.dot(left, right, precision=lax.Precision.HIGHEST, preferred_element_type=jnp.float32)


def on_device(trailing, leaf_v, leaf_t, merge_v, merge_t):
    panel = leaf_t.shape[0]
    vectors, triangle = (
        lax.all_gather(leaf_v, "cols", axis=1, tiled=True),
        lax.all_gather(leaf_t, "cols", axis=1, tiled=True),
    )
    triangle = jnp.triu(triangle)
    projected = mult(vectors.T, trailing)
    weights = mult(triangle.T, projected)
    block = trailing - mult(vectors, weights)
    top = block[:panel]
    remains = block[panel:]
    upper_a = merge_v[:panel]
    upper_b = merge_v[panel:]
    number = lax.axis_size("rows").bit_length() - 1
    position = lax.axis_index("rows")
    for level in range(number):
        stride = 1 << level
        is_upper = position % (2 * stride) == stride
        is_lower = position % (2 * stride) == 0
        outgoing = jnp.where(is_upper, mult(upper_b.T, top), top)
        incoming, got_a, got_t = partner((outgoing, upper_a, merge_t), "rows", level)
        use_a = jnp.where(is_upper, upper_a, got_a)
        use_factor = jnp.triu(jnp.where(is_upper, merge_t, got_t))
        first = mult(use_a.T, jnp.where(is_upper, incoming, top))
        summed = first + jnp.where(is_upper, outgoing, incoming)
        weight = mult(use_factor.T, summed)
        update_vec = jnp.where(is_upper, upper_b, use_a)
        new_top = top - mult(update_vec, weight)
        top = jnp.where(jnp.logical_or(is_upper, is_lower), new_top, top)
    return jnp.concatenate([top, remains], axis=0)


def solution(mesh):
    return jax.shard_map(
        on_device,
        mesh=mesh,
        in_specs=(
            P("rows", "cols"),
            P("rows", "cols"),
            P("rows", "cols"),
            P("rows", None),
            P("rows", None),
        ),
        out_specs=P("rows", "cols"),
        check_vma=False,
    )
```

profile of v0, /device:TPU:0, one launch (start us, length us, event | category | flops | bytes accessed | tf_op | source)
XLA Modules:
  0.0 490.5 jit_solution(4762212892131805072)
XLA Ops:
  6.5 0.0 all-gather.5.cloned.1.call-start
  6.5 0.7 all-gather.5.cloned.1.call-update
  7.3 0.0 all-gather.3.cloned.1.call-start
  7.3 0.7 all-gather.3.cloned.1.call-update
  8.0 26.5 %all-gather.5.cloned.1.call-done = f32[1024,512]{1,0:T(8,128)} async-done(((f32[1024,128]{1,0:T(8,128)}), f32[1024,512]{1,0:T(8,128)}) %all-gather.5.cloned.1.call-update) | async-done | bytes 2097168 | tf_op jit(solution)/shard_map/all_gather | solution.py:24
  34.5 9.6 %fusion.67 = f32[512,1024]{1,0:T(8,128)S(1)} fusion(f32[1024,512]{1,0:T(8,128)} %all-gather.5.cloned.1.call-done, f32[1024,1024]{1,0:T(8,128)} %param.5), kind=kOutput, calls=%fused_computation.78 | convolution fusion | flops 6442450944 | bytes 8388608 | tf_op jit(solution)/shard_map/dot_general | solution.py:18
  44.1 8.9 %all-gather.3.cloned.1.call-done = f32[512,512]{1,0:T(8,128)} async-done(((f32[512,128]{1,0:T(8,128)}), f32[512,512]{1,0:T(8,128)}) %all-gather.3.cloned.1.call-update) | async-done | bytes 1048592 | tf_op jit(solution)/shard_map/all_gather | solution.py:25
  52.9 0.0 copy-start.7
  52.9 5.0 %fusion.29 = f32[512,1024]{1,0:T(8,128)S(1)} fusion(f32[512,1024]{1,0:T(8,128)S(1)} %fusion.67, f32[512,512]{1,0:T(8,128)} %all-gather.3.cloned.1.call-done, s32[512]{0:T(512)S(1)} %iota_add_fusion), kind=kOutput, calls=%fused_computation.35 | convolution fusion | flops 3221749760 | bytes 5244928 | tf_op jit(solution)/shard_map/dot_general | solution.py:18
  57.9 0.0 copy-done.7
  57.9 0.0 copy-start
  57.9 9.2 %bitcast_subtract_fusion = f32[1024,1024]{1,0:T(8,128)S(1)} fusion(f32[1024,1024]{1,0:T(8,128)S(1)} %copy-done.7, f32[512,1024]{1,0:T(8,128)S(1)} %fusion.29, f32[1024,512]{1,0:T(8,128)} %all-gather.5.cloned.1.call-done), kind=kOutput, calls=%fused_computation.1 | convolution fusion | flops 6443499520 | bytes 12582912 | tf_op jit(solution)/shard_map/dot_general | solution.py:18
  67.1 0.0 copy-done
  67.1 0.0 copy-start.1
  67.1 5.4 %bitcast_select_fusion.2 = f32[512,1024]{1,0:T(8,128)} fusion(f32[1024,1024]{1,0:T(8,128)S(1)} %bitcast_subtract_fusion, pred[]{:T(512)S(6)} %eq.29, f32[1024,512]{1,0:T(8,128)S(1)} %copy-done), kind=kOutput, calls=%fused_computation.7 | convolution fusion | flops 3221749760 | bytes 7340033 | tf_op jit(solution)/shard_map/dot_general | solution.py:18
  72.5 0.0 copy-done.1
  72.5 0.0 copy-start.8
  72.5 1.5 collective-permute-start.2
  73.9 1.0 slice.14
  75.0 0.6 collective-permute-start
  75.5 0.0 copy-done.8
  75.5 1.5 collective-permute-start.1
  77.0 66.7 %collective-permute-done = f32[512,512]{1,0:T(8,128)} collective-permute-done((f32[512,512]{1,0:T(8,128)}, f32[512,512]{1,0:T(8,128)}, u32[]{:S(2)}, u32[]{:S(2)}) %collective-permute-start) | collective-permute-done | bytes 1048608 | tf_op jit(solution)/shard_map/ppermute | solution.py:14
  143.7 0.0 collective-permute-done.2
  143.7 5.7 %fusion.13 = f32[512,1024]{1,0:T(8,128)S(1)} fusion(f32[512,1024]{1,0:T(8,128)} %collective-permute-done.2, f32[1024,1024]{1,0:T(8,128)} %copy-done.1, pred[]{:T(512)S(6)} %eq.29, f32[512,512]{1,0:T(8,128)} %collective-permute-done, f32[1024,512]{1,0:T(8,128)S(1)} %copy-done), kind=kOutput, calls=%fused_computation.21 | convolution fusion | flops 3222011904 | bytes 8389632 | tf_op jit(solution)/shard_map/dot_general | solution.py:18
  149.4 0.0 copy-start.2
  149.4 16.1 %collective-permute-done.1 = f32[512,512]{1,0:T(8,128)} collective-permute-done((f32[512,512]{1,0:T(8,128)S(1)}, f32[512,512]{1,0:T(8,128)}, u32[]{:S(2)}, u32[]{:S(2)}) %collective-permute-start.1) | collective-permute-done | bytes 1048608 | tf_op jit(solution)/shard_map/ppermute | solution.py:14
  165.5 5.7 %fusion.10 = f32[512,1024]{1,0:T(8,128)S(1)} fusion(f32[512,1024]{1,0:T(8,128)S(1)} %fusion.13, f32[512,1024]{1,0:T(8,128)} %bitcast_select_fusion.2, f32[512,1024]{1,0:T(8,128)} %collective-permute-done.2, f32[512,512]{1,0:T(8,128)S(1)} %copy-done.8, f32[512,512]{1,0:T(8,128)} %collective-permute-done.1, pred[]{:T(512)S(6)} %eq.29, s32[512]{0:T(512)S(1)} %iota_add_fusion), kind=kOutput, calls=%fused_computation.18 | convolution fusion | flops 3223060480 | bytes 10487809 | tf_op jit(solution)/shard_map/dot_general | solution.py:18
  171.2 0.0 copy-done.2
  171.2 4.9 subtract_select_fusion.2
  176.1 0.0 copy-start.3
  176.1 4.9 bitcast_select_fusion.1
  181.0 0.0 copy-done.3
  181.0 1.5 collective-permute-start.5
  182.5 0.6 collective-permute-start.3
  183.0 1.5 collective-permute-start.4
  184.5 67.8 %collective-permute-done.3 = f32[512,512]{1,0:T(8,128)} collective-permute-done((f32[512,512]{1,0:T(8,128)}, f32[512,512]{1,0:T(8,128)}, u32[]{:S(2)}, u32[]{:S(2)}) %collective-permute-start.3) | collective-permute-done | bytes 1048608 | tf_op jit(solution)/shard_map/ppermute | solution.py:14
  252.3 0.0 collective-permute-done.5
  252.3 5.9 %fusion.8 = f32[512,1024]{1,0:T(8,128)S(1)} fusion(f32[512,1024]{1,0:T(8,128)} %collective-permute-done.5, f32[512,1024]{1,0:T(8,128)} %copy-done.3, pred[]{:T(512)S(6)} %eq.27, f32[512,512]{1,0:T(8,128)} %collective-permute-done.3, f32[1024,512]{1,0:T(8,128)S(1)} %copy-done), kind=kOutput, calls=%fused_computation.16 | convolution fusion | flops 3222011904 | bytes 8389632 | tf_op jit(solution)/shard_map/dot_general | solution.py:18
  258.2 0.0 copy-start.4
  258.2 15.0 %collective-permute-done.4 = f32[512,512]{1,0:T(8,128)} collective-permute-done((f32[512,512]{1,0:T(8,128)S(1)}, f32[512,512]{1,0:T(8,128)}, u32[]{:S(2)}, u32[]{:S(2)}) %collective-permute-start.4) | collective-permute-done | bytes 1048608 | tf_op jit(solution)/shard_map/ppermute | solution.py:14
  273.2 5.7 %fusion.5 = f32[512,1024]{1,0:T(8,128)S(1)} fusion(f32[512,1024]{1,0:T(8,128)S(1)} %fusion.8, f32[512,1024]{1,0:T(8,128)} %bitcast_select_fusion.1, f32[512,1024]{1,0:T(8,128)} %collective-permute-done.5, f32[512,512]{1,0:T(8,128)S(1)} %copy-done.8, f32[512,512]{1,0:T(8,128)} %collective-permute-done.4, pred[]{:T(512)S(6)} %eq.27, s32[512]{0:T(512)S(1)} %iota_add_fusion), kind=kOutput, calls=%fused_computation.13 | convolution fusion | flops 3223060480 | bytes 10487809 | tf_op jit(solution)/shard_map/dot_general | solution.py:18
  278.9 0.0 copy-done.4
  278.9 4.9 subtract_select_fusion.1
  283.8 0.0 copy-start.5
  283.8 4.9 bitcast_select_fusion
  288.7 0.0 copy-done.5
  288.7 2.4 collective-permute-start.8
  291.1 0.5 collective-permute-start.6
  291.6 2.4 collective-permute-start.7
  294.0 0.0 copy-start.6
  294.0 153.7 %collective-permute-done.6 = f32[512,512]{1,0:T(8,128)} collective-permute-done((f32[512,512]{1,0:T(8,128)}, f32[512,512]{1,0:T(8,128)}, u32[]{:S(2)}, u32[]{:S(2)}) %collective-permute-start.6) | collective-permute-done | bytes 1048608 | tf_op jit(solution)/shard_map/ppermute | solution.py:14
  447.8 0.0 collective-permute-done.8
  447.8 0.0 copy-done.6
  447.8 5.1 %fusion.3 = f32[512,1024]{1,0:T(8,128)S(1)} fusion(f32[512,1024]{1,0:T(8,128)} %collective-permute-done.8, f32[512,1024]{1,0:T(8,128)S(1)} %copy-done.6, pred[]{:T(512)S(6)} %eq.25, f32[512,512]{1,0:T(8,128)} %collective-permute-done.6, f32[1024,512]{1,0:T(8,128)S(1)} %copy-done), kind=kOutput, calls=%fused_computation.11 | convolution fusion | flops 3222011904 | bytes 8389632 | tf_op jit(solution)/shard_map/dot_general | solution.py:18
  452.9 17.3 %collective-permute-done.7 = f32[512,512]{1,0:T(8,128)} collective-permute-done((f32[512,512]{1,0:T(8,128)S(1)}, f32[512,512]{1,0:T(8,128)}, u32[]{:S(2)}, u32[]{:S(2)}) %collective-permute-start.7) | collective-permute-done | bytes 1048608 | tf_op jit(solution)/shard_map/ppermute | solution.py:14
  470.2 5.7 %fusion = f32[512,1024]{1,0:T(8,128)S(1)} fusion(f32[512,1024]{1,0:T(8,128)S(1)} %fusion.3, f32[512,1024]{1,0:T(8,128)} %bitcast_select_fusion, f32[512,1024]{1,0:T(8,128)} %collective-permute-done.8, f32[512,512]{1,0:T(8,128)S(1)} %copy-done.8, f32[512,512]{1,0:T(8,128)} %collective-permute-done.7, pred[]{:T(512)S(6)} %eq.25, s32[512]{0:T(512)S(1)} %iota_add_fusion), kind=kOutput, calls=%fused_computation.8 | convolution fusion | flops 3223060480 | bytes 10487809 | tf_op jit(solution)/shard_map/dot_general | solution.py:18
  475.8 0.0 slice-start
  475.8 5.1 %subtract_select_fusion = f32[512,1024]{1,0:T(8,128)S(1)} fusion(f32[512,1024]{1,0:T(8,128)S(1)} %copy-done.6, f32[512,1024]{1,0:T(8,128)S(1)} %fusion, pred[]{:T(512)S(6)} %or.9, f32[1024,512]{1,0:T(8,128)S(1)} %copy-done, pred[]{:T(512)S(6)} %eq.25, f32[512,512]{1,0:T(8,128)} %collective-permute-done.6), kind=kOutput, calls=%fused_computation.2 | convolution fusion | flops 3222798336 | bytes 9437186 | tf_op jit(solution)/shard_map/dot_general | solution.py:18
  480.9 0.0 slice-done
  480.9 2.5 pad_maximum_fusion
  (1 shorter events, 0.0 us)
Async XLA Ops:
  6.5 27.9 %all-gather.5.cloned.1.call-start = ((), (), s32[]{:S(2)}) async-start(), calls=%async_computation.1 | async-start | bytes 2621440 | tf_op jit(solution)/shard_map/all_gather | solution.py:24
  7.3 45.7 %all-gather.3.cloned.1.call-start = ((), (), s32[]{:S(2)}) async-start(), calls=%async_computation | async-start | bytes 1310720 | tf_op jit(solution)/shard_map/all_gather | solution.py:25
  52.9 5.0 %copy-start.7 = (f32[1024,1024]{1,0:T(8,128)S(1)}, f32[1024,1024]{1,0:T(8,128)}, u32[]{:S(2)}) copy-start(f32[1024,1024]{1,0:T(8,128)} %param.5) | copy-start | bytes 12582916
  57.9 9.2 %copy-start = (f32[1024,512]{1,0:T(8,128)S(1)}, f32[1024,512]{1,0:T(8,128)}, u32[]{:S(2)}) copy-start(f32[1024,512]{1,0:T(8,128)} %param.8) | copy-start | bytes 6291460
  67.1 5.4 %copy-start.1 = (f32[1024,1024]{1,0:T(8,128)}, f32[1024,1024]{1,0:T(8,128)S(1)}, u32[]{:S(2)}) copy-start(f32[1024,1024]{1,0:T(8,128)S(1)} %bitcast_subtract_fusion) | copy-start | bytes 12582916
  72.5 3.1 copy-start.8
  72.5 71.3 %collective-permute-start.2 = (f32[512,1024]{1,0:T(8,128)}, f32[512,1024]{1,0:T(8,128)}, u32[]{:S(2)}, u32[]{:S(2)}) collective-permute-start(f32[512,1024]{1,0:T(8,128)} %bitcast_select_fusion.2), channel_id=1, source_target_pairs={{0,4},{4,0},{8,12},{12,8},{16,20},{20,16},{24,28},{28,24},{1,5},{5... | collective-permute-start | bytes 6291464 | tf_op jit(solution)/shard_map/ppermute | solution.py:14
  75.0 68.8 %collective-permute-start = (f32[512,512]{1,0:T(8,128)}, f32[512,512]{1,0:T(8,128)}, u32[]{:S(2)}, u32[]{:S(2)}) collective-permute-start(f32[512,512]{1,0:T(8,128)} %slice.14), channel_id=1, source_target_pairs={{0,4},{4,0},{8,12},{12,8},{16,20},{20,16},{24,28},{28,24},{1,5},{5... | collective-permute-start | bytes 3145736 | tf_op jit(solution)/shard_map/ppermute | solution.py:14
  75.5 90.0 %collective-permute-start.1 = (f32[512,512]{1,0:T(8,128)S(1)}, f32[512,512]{1,0:T(8,128)}, u32[]{:S(2)}, u32[]{:S(2)}) collective-permute-start(f32[512,512]{1,0:T(8,128)S(1)} %copy-done.8), channel_id=1, source_target_pairs={{0,4},{4,0},{8,12},{12,8},{16,20},{20,16},{24,28},{28,24},{1,5},{5... | collective-permute-start | bytes 3145736 | tf_op jit(solution)/shard_map/ppermute | solution.py:14
  149.4 21.7 %copy-start.2 = (f32[1024,1024]{1,0:T(8,128)S(1)}, f32[1024,1024]{1,0:T(8,128)}, u32[]{:S(2)}) copy-start(f32[1024,1024]{1,0:T(8,128)} %copy-done.1) | copy-start | bytes 12582916
  176.1 4.9 %copy-start.3 = (f32[512,1024]{1,0:T(8,128)}, f32[512,1024]{1,0:T(8,128)S(1)}, u32[]{:S(2)}) copy-start(f32[512,1024]{1,0:T(8,128)S(1)} %subtract_select_fusion.2) | copy-start | bytes 6291460
  181.0 71.4 %collective-permute-start.5 = (f32[512,1024]{1,0:T(8,128)}, f32[512,1024]{1,0:T(8,128)}, u32[]{:S(2)}, u32[]{:S(2)}) collective-permute-start(f32[512,1024]{1,0:T(8,128)} %bitcast_select_fusion.1), channel_id=1, source_target_pairs={{0,8},{8,0},{4,12},{12,4},{16,24},{24,16},{20,28},{28,20},{1,9},{9... | collective-permute-start | bytes 6291464 | tf_op jit(solution)/shard_map/ppermute | solution.py:14
  182.5 69.9 %collective-permute-start.3 = (f32[512,512]{1,0:T(8,128)}, f32[512,512]{1,0:T(8,128)}, u32[]{:S(2)}, u32[]{:S(2)}) collective-permute-start(f32[512,512]{1,0:T(8,128)} %slice.14), channel_id=1, source_target_pairs={{0,8},{8,0},{4,12},{12,4},{16,24},{24,16},{20,28},{28,20},{1,9},{9... | collective-permute-start | bytes 3145736 | tf_op jit(solution)/shard_map/ppermute | solution.py:14
  183.0 90.2 %collective-permute-start.4 = (f32[512,512]{1,0:T(8,128)S(1)}, f32[512,512]{1,0:T(8,128)}, u32[]{:S(2)}, u32[]{:S(2)}) collective-permute-start(f32[512,512]{1,0:T(8,128)S(1)} %copy-done.8), channel_id=1, source_target_pairs={{0,8},{8,0},{4,12},{12,4},{16,24},{24,16},{20,28},{28,20},{1,9},{9... | collective-permute-start | bytes 3145736 | tf_op jit(solution)/shard_map/ppermute | solution.py:14
  258.2 20.6 %copy-start.4 = (f32[512,1024]{1,0:T(8,128)S(1)}, f32[512,1024]{1,0:T(8,128)}, u32[]{:S(2)}) copy-start(f32[512,1024]{1,0:T(8,128)} %copy-done.3) | copy-start | bytes 6291460
  283.8 4.9 %copy-start.5 = (f32[512,1024]{1,0:T(8,128)}, f32[512,1024]{1,0:T(8,128)S(1)}, u32[]{:S(2)}) copy-start(f32[512,1024]{1,0:T(8,128)S(1)} %subtract_select_fusion.1) | copy-start | bytes 6291460
  288.7 159.1 %collective-permute-start.8 = (f32[512,1024]{1,0:T(8,128)}, f32[512,1024]{1,0:T(8,128)}, u32[]{:S(2)}, u32[]{:S(2)}) collective-permute-start(f32[512,1024]{1,0:T(8,128)} %bitcast_select_fusion), channel_id=1, source_target_pairs={{0,16},{16,0},{4,20},{20,4},{8,24},{24,8},{12,28},{28,12},{1,17},{... | collective-permute-start | bytes 6291464 | tf_op jit(solution)/shard_map/ppermute | solution.py:14
  291.1 156.7 %collective-permute-start.6 = (f32[512,512]{1,0:T(8,128)}, f32[512,512]{1,0:T(8,128)}, u32[]{:S(2)}, u32[]{:S(2)}) collective-permute-start(f32[512,512]{1,0:T(8,128)} %slice.14), channel_id=1, source_target_pairs={{0,16},{16,0},{4,20},{20,4},{8,24},{24,8},{12,28},{28,12},{1,17},{... | collective-permute-start | bytes 3145736 | tf_op jit(solution)/shard_map/ppermute | solution.py:14
  291.6 178.5 %collective-permute-start.7 = (f32[512,512]{1,0:T(8,128)S(1)}, f32[512,512]{1,0:T(8,128)}, u32[]{:S(2)}, u32[]{:S(2)}) collective-permute-start(f32[512,512]{1,0:T(8,128)S(1)} %copy-done.8), channel_id=1, source_target_pairs={{0,16},{16,0},{4,20},{20,4},{8,24},{24,8},{12,28},{28,12},{1,17},{... | collective-permute-start | bytes 3145736 | tf_op jit(solution)/shard_map/ppermute | solution.py:14
  294.0 153.8 %copy-start.6 = (f32[512,1024]{1,0:T(8,128)S(1)}, f32[512,1024]{1,0:T(8,128)}, u32[]{:S(2)}) copy-start(f32[512,1024]{1,0:T(8,128)} %copy-done.5) | copy-start | bytes 6291460
  475.8 5.1 %slice-start = ((f32[1024,1024]{1,0:T(8,128)}), f32[512,1024]{1,0:T(8,128)S(1)}, s32[]{:S(2)}) async-start(f32[1024,1024]{1,0:T(8,128)} %copy-done.1), calls=%async_computation.2 | async-start | bytes 4194304 | tf_op jit(solution)/shard_map/slice | solution.py:32
Sparse Core Ops, SparseCore 0:
  8.9 25.5 all-gather.4
  36.0 16.8 all-gather.2
where the time goes:
time: 494 us; the launch traced here: 491 us
  waiting for transfers between devices  373 us (76%)
  matrix products  87.3 us (18%)
  between operations  13.9 us (3%)
  starting transfers between devices  12.4 us (3%)
    ppermute x9, waiting for transfers between devices, partner(): return lax.ppermute(block, axis, route)  337 us
    dot_general x15, matrix products, mult(): jnp.dot(left, right, precision=lax.Precision.HIGHEST, preferred_element_t...  87.3 us
    all_gather x1, waiting for transfers between devices, on_device(): lax.all_gather(leaf_v, 'cols', axis=1, tiled=True)  26.5 us
    ppermute x9, starting transfers between devices, partner(): return lax.ppermute(block, axis, route)  12.3 us
  transfers between devices with their start and end apart: 11, of which 8 were waited for; matrix products, arithmetic and copies ran while one was open for 6% of the time, Pallas kernels for 0%

commit v1 on v0

v1 whole, which is shorter than its diff:
```python
import functools

import jax
import jax.numpy as jnp
from jax import lax
from jax.experimental import pallas as pl
from jax.experimental.pallas import tpu as pltpu
from jax.sharding import PartitionSpec as P

F32 = jnp.float32
BF16 = jnp.bfloat16
MESH = pl.DeviceIdType.MESH
CHUNKS = 2


def split(x):
    high = x.astype(BF16)
    return high, (x - high.astype(F32)).astype(BF16)


def dot(a, b):
    return lax.dot_general(a, b, (((1,), (0,)), ((), ())), preferred_element_type=F32)


def mult(ah, al, x):
    bh, bl = split(x)
    return dot(ah, bh) + (dot(ah, bl) + dot(al, bh))


def triu(x):
    row = lax.broadcasted_iota(jnp.int32, x.shape, 0)
    col = lax.broadcasted_iota(jnp.int32, x.shape, 1)
    return jnp.where(row <= col, x, 0.0)


def kernel(nr, tr, lv, lt, mv, mt, out, vb, tb, cb, ab, m0, mg, ml, buf, snd, pk, xs, ys,
           vt, vs, ltt, at, an, m0t, gt, gn, mlt,
           loc, gs, gr, ps, xsend, xrecv, lsend, lrecv, rsend, rrecv):
    levels = nr.bit_length() - 1
    m, p = vb.shape
    n = cb.shape[1]
    half = n // 2
    tc = half // CHUNKS
    tiles = 2 * CHUNKS
    q = lv.shape[1]
    r = lax.axis_index("rows")
    c = lax.axis_index("cols")
    par = r % 2
    mate = r + 1 - 2 * par
    yc = c + 2 - 4 * (c // 2)
    cc = c + 1 - 2 * (c % 2)

    barrier = pltpu.get_barrier_semaphore()
    for step in range(1, nr):
        pl.semaphore_signal(barrier, inc=1, device_id=((r + step) % nr, c), device_id_type=MESH)
    for col in (yc, cc):
        pl.semaphore_signal(barrier, inc=1, device_id=(r, col), device_id_type=MESH)

    def remote(src, dst, send, recv, row, col):
        return pltpu.make_async_remote_copy(src_ref=src, dst_ref=dst, send_sem=send, recv_sem=recv,
                                            device_id=(row, col), device_id_type=MESH)

    def cols_of(k):
        return pl.ds(pl.multiple_of(k * q, q), q)

    items = [lambda k: vb.at[:, cols_of(k)], lambda k: tb.at[:, cols_of(k)],
             lambda k: ab.at[:, cols_of(k)], lambda k: m0.at[cols_of(k)]]
    for l in range(1, levels):
        items.append(functools.partial(lambda l, k: mg.at[l - 1, cols_of(k)], l))
        items.append(functools.partial(lambda l, k: ml.at[l - 1, cols_of(k)], l))

    def y_copy(i, src=None):
        return remote(items[i](c) if src is None else src, items[i](c), gs.at[i, 0], gr.at[i, 0], r, yc)

    def own_copy(i, src=None):
        return remote(items[i](c) if src is None else src, items[i](c), gs.at[i, 1], gr.at[i, 1], r, cc)

    def fwd_copy(i):
        return remote(items[i](yc), items[i](yc), gs.at[i, 2], gr.at[i, 2], r, cc)

    def in_wait(i):
        remote(items[i](c), items[i](c), gs.at[i, 0], gr.at[i, 3], r, c).wait_recv()

    def forward(i):
        y_copy(i).wait_recv()
        fwd_copy(i).start()

    def stride(l):
        return 1 << l

    def active(l):
        return r % stride(l) < 2

    def upper(l):
        return (r // stride(l)) % 2 == 1

    def holder(l):
        return r % stride(l + 1) == stride(l)

    def needs(l):
        return jnp.logical_and(active(l), jnp.logical_not(holder(l)))

    trail_in = pltpu.make_async_copy(tr, cb, loc.at[0])
    v_in = pltpu.make_async_copy(lv, items[0](c), loc.at[1])
    t_in = pltpu.make_async_copy(lt, items[1](c), loc.at[2])
    v_in.start()
    trail_in.start()
    t_in.start()
    ab_in = pltpu.make_async_copy(mv, ab, loc.at[3])
    m_in = pltpu.make_async_copy(mt, m0, loc.at[4])

    pl.semaphore_wait(barrier, nr + 1)
    own_copy(0, lv).start()
    y_copy(0, lv).start()
    own_copy(1, lt).start()
    y_copy(1, lt).start()

    def first_sends():
        return [remote(mv.at[:, cols_of(c)], ab.at[:, cols_of(c)], ps.at[0, 0], gr.at[2, 3], mate, c),
                remote(mt.at[cols_of(c)], m0.at[cols_of(c)], ps.at[0, 1], gr.at[3, 3], mate, c)]

    def level_sends(l):
        i = 2 + 2 * l
        sends = []
        for k, (row, side) in enumerate(((r - stride(l), 0), (r - stride(l) + 1, 0), (r + 1, 1))):
            sends.append(remote(mv.at[side, cols_of(c)], mg.at[l - 1, cols_of(c)],
                                ps.at[l, 2 * k], gr.at[i, 3], row, c))
            sends.append(remote(mt.at[cols_of(c)], ml.at[l - 1, cols_of(c)],
                                ps.at[l, 2 * k + 1], gr.at[i + 1, 3], row, c))
        return sends

    def own_level(l):
        return [pltpu.make_async_copy(mv.at[1], mg.at[l - 1], loc.at[3]),
                pltpu.make_async_copy(mt, ml.at[l - 1], loc.at[4])]

    @pl.when(par == 1)
    def _():
        for copy in first_sends():
            copy.start()
        ab_in.start()
        m_in.start()

    for l in range(1, levels):
        @pl.when(holder(l))
        def _(l=l):
            for copy in level_sends(l) + own_level(l):
                copy.start()

    def place(s):
        sent = s < CHUNKS
        chunk = jnp.where(sent, s, s - CHUNKS)
        side = jnp.where(sent, 1 - par, par)
        return pl.ds(pl.multiple_of(side * half + chunk * tc, tc), tc)

    def project(block):
        rows = pl.ds(pl.multiple_of(block * 2 * q, 2 * q), 2 * q)
        piece = vb[:, rows]
        high, low = split(piece)
        vs[0, :, rows] = high
        vs[1, :, rows] = low
        high, low = split(piece.T)
        vt[0, rows] = high
        vt[1, rows] = low

        def body(s, _):
            pk[s, rows] = mult(vt[0, rows], vt[1, rows], cb[:, place(s)])
            return 0

        lax.fori_loop(0, tiles, body, 0)

    v_in.wait()
    own_copy(0).wait_recv()
    trail_in.wait()
    project(c // 2)
    forward(0)
    fwd_copy(0).wait_recv()
    project(1 - c // 2)
    forward(1)

    @pl.when(par == 0)
    def _():
        for i in (2, 3):
            in_wait(i)
            y_copy(i).start()
            own_copy(i).start()

    t_in.wait()
    own_copy(1).wait_recv()
    fwd_copy(1).wait_recv()
    high, low = split(triu(tb[...]).T)
    ltt[0] = high
    ltt[1] = low

    def swap(ch):
        return remote(snd.at[ch], buf.at[par, ch], lsend.at[ch], lrecv.at[ch], mate, c)

    def leaf(s, dest):
        weights = mult(ltt[0], ltt[1], pk[s])
        pk[s] = weights
        dest[...] = cb[:p, place(s)] - mult(vs[0, :p], vs[1, :p], weights)

    def leaf_sent(ch, _):
        leaf(ch, snd.at[ch])
        swap(ch).start()
        return 0

    def leaf_kept(ch, _):
        leaf(ch + CHUNKS, buf.at[par, ch])
        return 0

    lax.fori_loop(0, CHUNKS, leaf_sent, 0)
    lax.fori_loop(0, CHUNKS, leaf_kept, 0)

    @pl.when(par == 0)
    def _():
        forward(2)
        forward(3)

    for l in range(1, levels):
        @pl.when(needs(l))
        def _(l=l):
            for i in (2 + 2 * l, 3 + 2 * l):
                in_wait(i)
                y_copy(i).start()
                own_copy(i).start()

    def remains(s, _):
        cb[p:, place(s)] = cb[p:, place(s)] - mult(vs[0, p:], vs[1, p:], pk[s])
        return 0

    lax.fori_loop(0, tiles, remains, 0)
    rest_out = pltpu.make_async_copy(cb.at[pl.ds(p, m - p)], out.at[pl.ds(p, m - p)], loc.at[0])
    rest_out.start()

    @pl.when(par == 0)
    def _():
        for i in (2, 3):
            own_copy(i).wait_recv()
            fwd_copy(i).wait_recv()

    @pl.when(par == 1)
    def _():
        ab_in.wait()
        m_in.wait()

    def prepare(k, _):
        an[k, 0], an[k, 1] = split(ab[k])
        at[k, 0], at[k, 1] = split(ab[k].T)
        return 0

    lax.fori_loop(0, 2, prepare, 0)
    m0t[0], m0t[1] = split(triu(m0[...]).T)

    def level_ready(l):
        @pl.when(needs(l))
        def _():
            for i in (2 + 2 * l, 3 + 2 * l):
                forward(i)
            for i in (2 + 2 * l, 3 + 2 * l):
                own_copy(i).wait_recv()
                fwd_copy(i).wait_recv()

        @pl.when(holder(l))
        def _():
            for copy in own_level(l):
                copy.wait()

        @pl.when(active(l))
        def _():
            gn[l - 1, 0], gn[l - 1, 1] = split(mg[l - 1])
            gt[l - 1, 0], gt[l - 1, 1] = split(mg[l - 1].T)
            mlt[l - 1, 0], mlt[l - 1, 1] = split(triu(ml[l - 1]).T)

    def exchange(l, ch):
        partner = r + stride(l) - 2 * stride(l) * ((r // stride(l)) % 2)
        return remote(xs.at[l - 1, ch], ys.at[l - 1, ch], xsend.at[l - 1, ch], xrecv.at[l - 1, ch], partner, c)

    def out_of(side, ch):
        return out.at[pl.ds(0, p), pl.ds(pl.multiple_of(side * half + ch * tc, tc), tc)]

    def give(k, ch):
        return remote(buf.at[k, ch], out_of(1 - k, ch), rsend.at[k, ch], rrecv.at[k, ch], mate, c)

    def keep(k, ch):
        return pltpu.make_async_copy(buf.at[k, ch], out_of(k, ch), rsend.at[k, ch])

    def finish(k, ch):
        @pl.when(par == k)
        def _():
            keep(k, ch).start()

        @pl.when(par != k)
        def _():
            give(k, ch).start()

    def leave(l, ch):
        if l == levels:
            finish(0, ch)
            return

        @pl.when(active(l))
        def _():
            xs[l - 1, ch] = mult(gt[l - 1, 0], gt[l - 1, 1], buf[0, ch])
            exchange(l, ch).start()

    def first(ch, _):
        swap(ch).wait_recv()
        total = mult(at[0, 0], at[0, 1], buf[0, ch]) + mult(at[1, 0], at[1, 1], buf[1, ch])
        weights = mult(m0t[0], m0t[1], total)
        wh, wl = split(weights)
        for k in (1, 0):
            high, low = an[k, 0], an[k, 1]
            buf[k, ch] = buf[k, ch] - (dot(high, wh) + (dot(high, wl) + dot(low, wh)))
            if k:
                finish(1, ch)
        leave(1, ch)
        return 0

    if levels > 1:
        level_ready(1)
    lax.fori_loop(0, CHUNKS, first, 0)

    for l in range(1, levels):
        if l + 1 < levels:
            level_ready(l + 1)

        def merge(ch, _, l=l):
            exchange(l, ch).wait_recv()
            weights = mult(mlt[l - 1, 0], mlt[l - 1, 1], xs[l - 1, ch] + ys[l - 1, ch])
            buf[0, ch] = buf[0, ch] - mult(gn[l - 1, 0], gn[l - 1, 1], weights)

            @pl.when(upper(l))
            def _():
                finish(0, ch)

            @pl.when(jnp.logical_not(upper(l)))
            def _():
                leave(l + 1, ch)
            return 0

        @pl.when(active(l))
        def _(merge=merge):
            lax.fori_loop(0, CHUNKS, merge, 0)

    rest_out.wait()
    for i in (0, 1):
        y_copy(i).wait_send()
        own_copy(i).wait_send()
        fwd_copy(i).wait_send()

    @pl.when(par == 1)
    def _():
        for copy in first_sends():
            copy.wait_send()

    @pl.when(par == 0)
    def _():
        for i in (2, 3):
            y_copy(i).wait_send()
            own_copy(i).wait_send()
            fwd_copy(i).wait_send()

    for l in range(1, levels):
        @pl.when(holder(l))
        def _(l=l):
            for copy in level_sends(l):
                copy.wait_send()

        @pl.when(needs(l))
        def _(l=l):
            for i in (2 + 2 * l, 3 + 2 * l):
                y_copy(i).wait_send()
                own_copy(i).wait_send()
                fwd_copy(i).wait_send()

        @pl.when(active(l))
        def _(l=l):
            for ch in range(CHUNKS):
                exchange(l, ch).wait_send()

    for ch in range(CHUNKS):
        swap(ch).wait_send()
        for k in (0, 1):
            @pl.when(par == k)
            def _(k=k, ch=ch):
                keep(k, ch).wait()
                remote(buf.at[k, ch], out_of(1 - k, ch), rsend.at[k, ch], rrecv.at[k, ch], mate, c).wait_recv()

            @pl.when(par != k)
            def _(k=k, ch=ch):
                give(k, ch).wait_send()


def on_device(nr, nc, trailing, leaf_v, leaf_t, merge_v, merge_t):
    m, n = trailing.shape
    p = merge_t.shape[1]
    levels = nr.bit_length() - 1
    more = max(levels - 1, 1)
    tc = n // 2 // CHUNKS
    n_items = 2 + 2 * levels
    assert nc == 4 and nr == 1 << levels and levels > 0
    vmem = pltpu.VMEM
    sem = pltpu.SemaphoreType.DMA
    call = pl.pallas_call(
        functools.partial(kernel, nr),
        out_shape=jax.ShapeDtypeStruct((m, n), F32),
        in_specs=[pl.BlockSpec(memory_space=pl.ANY)] * 5,
        out_specs=pl.BlockSpec(memory_space=pl.ANY),
        scratch_shapes=[
            vmem((m, p), F32), vmem((p, p), F32), vmem((m, n), F32),
            vmem((2, p, p), F32), vmem((p, p), F32),
            vmem((more, p, p), F32), vmem((more, p, p), F32),
            vmem((2, CHUNKS, p, tc), F32), vmem((CHUNKS, p, tc), F32),
            vmem((2 * CHUNKS, p, tc), F32),
            vmem((more, CHUNKS, p, tc), F32), vmem((more, CHUNKS, p, tc), F32),
            vmem((2, p, m), BF16), vmem((2, m, p), BF16), vmem((2, p, p), BF16),
            vmem((2, 2, p, p), BF16), vmem((2, 2, p, p), BF16), vmem((2, p, p), BF16),
            vmem((more, 2, p, p), BF16), vmem((more, 2, p, p), BF16), vmem((more, 2, p, p), BF16),
            sem((5,)), sem((n_items, 3)), sem((n_items, 4)), sem((levels, 6)),
            sem((more, CHUNKS)), sem((more, CHUNKS)), sem((CHUNKS,)), sem((CHUNKS,)),
            sem((2, CHUNKS)), sem((2, CHUNKS)),
        ],
        compiler_params=pltpu.CompilerParams(
            collective_id=0, has_side_effects=True, vmem_limit_bytes=60 << 20),
        cost_estimate=pl.CostEstimate(
            flops=2 * n * p * (3 * m + 3 * p * levels), bytes_accessed=4 * (2 * m * n + 4 * m * p), transcendentals=0),
    )
    return call(trailing, leaf_v, leaf_t, merge_v.reshape(2, p, p), merge_t)


def solution(mesh):
    return jax.shard_map(
        functools.partial(on_device, mesh.shape["rows"], mesh.shape["cols"]),
        mesh=mesh,
        in_specs=(
            P("rows", "cols"),
            P("rows", "cols"),
            P("rows", "cols"),
            P("rows", None),
            P("rows", None),
        ),
        out_specs=P("rows", "cols"),
        check_vma=False,
    )
```

time: 494 us -> 134 us (0.27)
  waiting for transfers between devices: 373 us -> 0 us
  Pallas kernels: 0 us -> 129 us
  matrix products: 87.3 us -> 0 us
  between operations: 13.9 us -> 0.01 us
  starting transfers between devices: 12.4 us -> 0 us
    ppermute x9 -> x0, waiting for transfers between devices: 337 us -> none  [partner(): return lax.ppermute(block, axis, route)]
    pallas_call x0 -> x1, Pallas kernels: none -> 129 us  [on_device(): return call(trailing, leaf_v, leaf_t, merge_v.reshape(2, p, p), merge_t)]
    dot_general x15 -> x0, matrix products: 87.3 us -> none  [mult(): jnp.dot(left, right, precision=lax.Precision.HIGHEST, preferred_element_t...]
    all_gather x2 -> x0, waiting for transfers between devices: 35.3 us -> none  [the longest x1 26.5 us: on_device(): lax.all_gather(leaf_v, 'cols', axis=1, tiled=True)]
    ppermute x9 -> x0, starting transfers between devices: 12.3 us -> none  [partner(): return lax.ppermute(block, axis, route)]
  transfers between devices with their start and end apart: 11 -> 0, of which waited for: 8 -> 0; matrix products, arithmetic and copies ran while one was open for 6% -> 0% of each run, Pallas kernels for 0% -> 0%
where the time goes in v1:
time: 134 us
  Pallas kernels  129 us (96%)
  local copies, waits for them, and re-layouts  4.79 us (4%)
    pallas_call x1, Pallas kernels, on_device(): return call(trailing, leaf_v, leaf_t, merge_v.reshape(2, p, p), merge_t)  129 us
    unnamed x1, local copies, waits for them, and re-layouts  4.79 us

profile of v1, /device:TPU:0, one launch (start us, length us, event | category | flops | bytes accessed | tf_op | source)
XLA Modules:
  0.0 133.8 jit_solution(2525467370503246111)
XLA Ops:
  0.0 129.0 %shard_map.55 = f32[1024,1024]{1,0:T(8,128)} custom-call(f32[1024,1024]{1,0:T(8,128)} %tr.1, f32[1024,128]{1,0:T(8,128)} %lv.1, f32[512,128]{1,0:T(8,128)} %lt.1, f32[2,512,512]{2,1,0:T(8,128)} %bitcast.1, f32[512,512]{1,0:T(8,128)} %mt.1), custom_call_target="tpu_custom_call" | custom-call | flops 8053063680 | bytes 16777216 | tf_op jit(solution)/shard_map/pallas_call | solution.py:428
  129.0 4.8 %copy.7 = f32[1024,1024]{1,0:T(8,128)} copy(f32[1024,1024]{1,0:T(8,128)} %shard_map.55) | data formatting | bytes 8388608

commit v2 on v1

--- a/solution.py
+++ b/solution.py
@@ -10,7 +10,8 @@
 F32 = jnp.float32
 BF16 = jnp.bfloat16
 MESH = pl.DeviceIdType.MESH
-CHUNKS = 2
+CHUNKS = 4
+WIDE = 2
 
 
 def split(x):
@@ -41,7 +42,8 @@
     n = cb.shape[1]
     half = n // 2
     tc = half // CHUNKS
-    tiles = 2 * CHUNKS
+    tw = tc * WIDE
+    tiles = n // tw
     q = lv.shape[1]
     r = lax.axis_index("rows")
     c = lax.axis_index("cols")
@@ -129,9 +131,10 @@
                                 ps.at[l, 2 * k + 1], gr.at[i + 1, 3], row, c))
         return sends
 
-    def own_level(l):
-        return [pltpu.make_async_copy(mv.at[1], mg.at[l - 1], loc.at[3]),
-                pltpu.make_async_copy(mt, ml.at[l - 1], loc.at[4])]
+    def own_level(l, which):
+        if which == 0:
+            return pltpu.make_async_copy(mv.at[1], mg.at[l - 1], loc.at[3])
+        return pltpu.make_async_copy(mt, ml.at[l - 1], loc.at[4])
 
     @pl.when(par == 1)
     def _():
@@ -143,14 +146,14 @@
     for l in range(1, levels):
         @pl.when(holder(l))
         def _(l=l):
-            for copy in level_sends(l) + own_level(l):
+            for copy in level_sends(l) + [own_level(l, 0), own_level(l, 1)]:
                 copy.start()
 
     def place(s):
-        sent = s < CHUNKS
-        chunk = jnp.where(sent, s, s - CHUNKS)
+        sent = s < tiles // 2
+        tile = jnp.where(sent, s, s - tiles // 2)
         side = jnp.where(sent, 1 - par, par)
-        return pl.ds(pl.multiple_of(side * half + chunk * tc, tc), tc)
+        return pl.ds(pl.multiple_of(side * half + tile * tw, tw), tw)
 
     def project(block):
         rows = pl.ds(pl.multiple_of(block * 2 * q, 2 * q), 2 * q)
@@ -194,22 +197,26 @@
     def swap(ch):
         return remote(snd.at[ch], buf.at[par, ch], lsend.at[ch], lrecv.at[ch], mate, c)
 
-    def leaf(s, dest):
+    def leaf(s):
         weights = mult(ltt[0], ltt[1], pk[s])
         pk[s] = weights
-        dest[...] = cb[:p, place(s)] - mult(vs[0, :p], vs[1, :p], weights)
-
-    def leaf_sent(ch, _):
-        leaf(ch, snd.at[ch])
-        swap(ch).start()
-        return 0
-
-    def leaf_kept(ch, _):
-        leaf(ch + CHUNKS, buf.at[par, ch])
-        return 0
-
-    lax.fori_loop(0, CHUNKS, leaf_sent, 0)
-    lax.fori_loop(0, CHUNKS, leaf_kept, 0)
+        return cb[:p, place(s)] - mult(vs[0, :p], vs[1, :p], weights)
+
+    def leaf_sent(t, _):
+        top = leaf(t)
+        for k in range(WIDE):
+            snd[t * WIDE + k] = top[:, k * tc:(k + 1) * tc]
+            swap(t * WIDE + k).start()
+        return 0
+
+    def leaf_kept(t, _):
+        top = leaf(t + tiles // 2)
+        for k in range(WIDE):
+            buf[par, t * WIDE + k] = top[:, k * tc:(k + 1) * tc]
+        return 0
+
+    lax.fori_loop(0, tiles // 2, leaf_sent, 0)
+    lax.fori_loop(0, tiles // 2, leaf_kept, 0)
 
     @pl.when(par == 0)
     def _():
@@ -251,24 +258,30 @@
     lax.fori_loop(0, 2, prepare, 0)
     m0t[0], m0t[1] = split(triu(m0[...]).T)
 
-    def level_ready(l):
+    def arrived(i, l, which):
         @pl.when(needs(l))
         def _():
-            for i in (2 + 2 * l, 3 + 2 * l):
-                forward(i)
-            for i in (2 + 2 * l, 3 + 2 * l):
-                own_copy(i).wait_recv()
-                fwd_copy(i).wait_recv()
+            forward(i)
+            own_copy(i).wait_recv()
+            fwd_copy(i).wait_recv()
 
         @pl.when(holder(l))
         def _():
-            for copy in own_level(l):
-                copy.wait()
+            own_level(l, which).wait()
+
+    def vectors_ready(l):
+        arrived(2 + 2 * l, l, 0)
 
         @pl.when(active(l))
         def _():
+            gt[l - 1, 0], gt[l - 1, 1] = split(mg[l - 1].T)
             gn[l - 1, 0], gn[l - 1, 1] = split(mg[l - 1])
-            gt[l - 1, 0], gt[l - 1, 1] = split(mg[l - 1].T)
+
+    def triangle_ready(l):
+        arrived(3 + 2 * l, l, 1)
+
+        @pl.when(active(l))
+        def _():
             mlt[l - 1, 0], mlt[l - 1, 1] = split(triu(ml[l - 1]).T)
 
     def exchange(l, ch):
@@ -311,18 +324,23 @@
         for k in (1, 0):
             high, low = an[k, 0], an[k, 1]
             buf[k, ch] = buf[k, ch] - (dot(high, wh) + (dot(high, wl) + dot(low, wh)))
-            if k:
-                finish(1, ch)
         leave(1, ch)
         return 0
 
     if levels > 1:
-        level_ready(1)
+        vectors_ready(1)
     lax.fori_loop(0, CHUNKS, first, 0)
 
+    def home(ch, _):
+        finish(1, ch)
+        return 0
+
+    lax.fori_loop(0, CHUNKS, home, 0)
+
     for l in range(1, levels):
+        triangle_ready(l)
         if l + 1 < levels:
-            level_ready(l + 1)
+            vectors_ready(l + 1)
 
         def merge(ch, _, l=l):
             exchange(l, ch).wait_recv()
@@ -411,7 +429,7 @@
             vmem((2, p, p), F32), vmem((p, p), F32),
             vmem((more, p, p), F32), vmem((more, p, p), F32),
             vmem((2, CHUNKS, p, tc), F32), vmem((CHUNKS, p, tc), F32),
-            vmem((2 * CHUNKS, p, tc), F32),
+            vmem((n // (WIDE * tc), p, WIDE * tc), F32),
             vmem((more, CHUNKS, p, tc), F32), vmem((more, CHUNKS, p, tc), F32),
             vmem((2, p, m), BF16), vmem((2, m, p), BF16), vmem((2, p, p), BF16),
             vmem((2, 2, p, p), BF16), vmem((2, 2, p, p), BF16), vmem((2, p, p), BF16),

time: 134 us -> 129 us (0.963)
  Pallas kernels: 129 us -> 124 us
    pallas_call x1, Pallas kernels: 129 us -> 124 us  [on_device(): return call(trailing, leaf_v, leaf_t, merge_v.reshape(2, p, p), merge_t)]
where the time goes in v2:
time: 129 us
  Pallas kernels  124 us (96%)
  local copies, waits for them, and re-layouts  4.79 us (4%)
    pallas_call x1, Pallas kernels, on_device(): return call(trailing, leaf_v, leaf_t, merge_v.reshape(2, p, p), merge_t)  124 us
    unnamed x1, local copies, waits for them, and re-layouts  4.79 us

profile of v2, /device:TPU:0, one launch (start us, length us, event | category | flops | bytes accessed | tf_op | source)
XLA Modules:
  0.0 128.6 jit_solution(17790463335966524757)
XLA Ops:
  0.0 123.8 %shard_map.55 = f32[1024,1024]{1,0:T(8,128)} custom-call(f32[1024,1024]{1,0:T(8,128)} %tr.1, f32[1024,128]{1,0:T(8,128)} %lv.1, f32[512,128]{1,0:T(8,128)} %lt.1, f32[2,512,512]{2,1,0:T(8,128)} %bitcast.1, f32[512,512]{1,0:T(8,128)} %mt.1), custom_call_target="tpu_custom_call" | custom-call | flops 8053063680 | bytes 16777216 | tf_op jit(solution)/shard_map/pallas_call | solution.py:446
  123.9 4.8 %copy.7 = f32[1024,1024]{1,0:T(8,128)} copy(f32[1024,1024]{1,0:T(8,128)} %shard_map.55) | data formatting | bytes 8388608
